TPU v7x, 1024 devices: a whole 4x8x16 slice. The times are simulated.
1024 devices in a mesh: ctx: 64 (over y, z_lo), tp: 16 (over x, z_hi, core).
Axes of the slice: x: 4, y: 8, z: 16 (z_hi: 2, z_lo: 8; z = z_hi * 8 + z_lo), core: 2. Of those that a mesh axis runs over, the one named last changes fastest.
Arguments:
- queries: bfloat16 [8192, 8192], P('ctx', 'tp'), may hold values from -6 to 6
- keys: bfloat16 [8192, 8192], P('ctx', 'tp'), may hold values from -6 to 6
- values: bfloat16 [8192, 8192], P('ctx', 'tp'), may hold values from -6 to 6
- short_taps: float32 [3, 3, 8192], P(None, None, 'tp'), may hold values from -3.5 to 3.5
- long_rates: float32 [8192, 16], P('tp'), may hold values from 2.4414062e-06 to 0.05
- long_resid: float32 [8192, 16], P('tp'), may hold values from -1.5 to 1.5
- out_weight: bfloat16 [8192, 4096], P('tp'), may hold values from -0.09375 to 0.09375
Outputs:
- block_out: bfloat16 [8192, 4096], P('ctx', 'tp')
All inputs are finite; a program needn't handle non-finite values.
Results may differ from a plain program's by a relative error of at most 0.017.
Values may be sent and summed in bfloat16 or wider, within the bound.
A program may use at most 128 MiB of HBM per device.

v0:
```python
import math

import jax
import jax.numpy as jnp
from jax import lax
from jax.sharding import PartitionSpec as P


def shifted(value, axis, steps):
    count = lax.axis_size(axis)
    initial, last = (max(0, -steps), min(count, count - steps))
    return lax.ppermute(value, axis, [(source, source + steps) for source in range(initial, last)])


def causal_taps(stream, leading, filter_taps):
    tok_rows = stream.shape[0]
    tail_len = filter_taps.shape[0] - 1
    extended = jnp.concatenate([leading, stream], axis=0).astype(jnp.float32)
    accum_sum = jnp.zeros(stream.shape, jnp.float32)
    for tap_index in range(filter_taps.shape[0]):
        accum_sum = (
            accum_sum
            + filter_taps[tap_index]
            * extended[tail_len - tap_index : tail_len - tap_index + tok_rows]
        )
    return accum_sum


def by_groups(inner_fn, arrays):
    channels = arrays[0].shape[0]
    group = math.gcd(channels, 128)
    stacked = tuple((item.reshape((channels // group, group) + item.shape[1:]) for item in arrays))
    result = lax.map(lambda pieces: inner_fn(*pieces), stacked)
    return result.reshape((channels,) + result.shape[2:])


def modal_conv(signal, decay_rates, residues, state_start):
    better = lax.Precision.HIGH
    channels, length = signal.shape
    block_len = math.gcd(length, 256)
    num_blocks = length // block_len
    mode_gain = residues * jnp.sqrt(-jnp.expm1(-2.0 * decay_rates))
    positions = jnp.arange(block_len, dtype=jnp.float32)
    grow_pow = jnp.exp(-decay_rates[:, None, :] * positions[None, :, None])
    left_side = grow_pow * mode_gain[:, None, :]
    kernel = jnp.sum(left_side, axis=2)
    row_index = jnp.arange(block_len, dtype=jnp.int32)
    offset_table = row_index[:, None] - row_index[None, :]
    causal_mask = offset_table >= 0
    toeplitz = jnp.take(kernel, jnp.maximum(offset_table, 0), axis=1)
    toeplitz = jnp.where(causal_mask[None], toeplitz, 0.0)
    blocks_in = signal.reshape(channels, num_blocks, block_len)
    inner_part = jnp.einsum("cij,cbj->cbi", toeplitz, blocks_in, precision=better)
    tail_pow = jnp.exp(-decay_rates[:, None, :] * (block_len - 1.0 - positions)[None, :, None])
    block_ends = jnp.einsum("cbj,cjm->cbm", blocks_in, tail_pow, precision=better)
    block_idx = jnp.arange(num_blocks, dtype=jnp.float32)
    gap_count = block_idx[:, None] - block_idx[None, :] - 1.0
    carry_decay = jnp.exp(
        -decay_rates[:, :, None, None] * block_len * jnp.maximum(gap_count, 0.0)[None, None]
    )
    carry_decay = jnp.where((gap_count >= 0.0)[None, None], carry_decay, 0.0)
    states = jnp.einsum("cmbk,ckm->cbm", carry_decay, block_ends, precision=better)
    states = (
        states
        + jnp.exp(-decay_rates[:, None, :] * (block_len * block_idx)[None, :, None])
        * state_start[:, None, :]
    )
    after_one = left_side * jnp.exp(-decay_rates)[:, None, :]
    outer_part = jnp.einsum("cim,cbm->cbi", after_one, states, precision=better)
    return (inner_part + outer_part).reshape(channels, length)


def shards(queries, keys, values, short_taps, long_rates, long_resid, out_weight):
    tok_rows, channels = queries.shape
    tail_len = short_taps.shape[1] - 1
    leading = shifted(
        (
            queries[tok_rows - tail_len :],
            keys[tok_rows - tail_len :],
            values[tok_rows - tail_len :],
        ),
        "ctx",
        1,
    )
    q_feat = causal_taps(queries, leading[0], short_taps[0])
    k_feat = causal_taps(keys, leading[1], short_taps[1])
    v_feat = causal_taps(values, leading[2], short_taps[2])
    product = (k_feat * v_feat).astype(jnp.bfloat16)
    modes = long_rates.shape[1]
    channel_share = channels // lax.axis_size("ctx")
    turned = lax.all_to_all(product.T, "ctx", split_axis=0, concat_axis=1, tiled=True)
    first_row = lax.axis_index("ctx") * channel_share
    rate_slice = lax.dynamic_slice_in_dim(long_rates, first_row, channel_share, 0)
    resid_slice = lax.dynamic_slice_in_dim(long_resid, first_row, channel_share, 0)
    zero_state = jnp.zeros((channel_share, modes), jnp.float32)
    filtered = by_groups(
        modal_conv, (turned.astype(jnp.float32), rate_slice, resid_slice, zero_state)
    ).astype(jnp.bfloat16)
    long_out = lax.all_to_all(filtered, "ctx", split_axis=1, concat_axis=0, tiled=True).T
    long_out = lax.optimization_barrier(long_out)
    gated = (q_feat * long_out.astype(jnp.float32)).astype(jnp.bfloat16)
    summed_rows = lax.psum_scatter(
        lax.dot_general(
            out_weight, gated, (((0,), (1,)), ((), ())), preferred_element_type=jnp.float32
        ).astype(jnp.bfloat16),
        "tp",
        scatter_dimension=0,
        tiled=True,
    ).astype(jnp.float32)
    return summed_rows.T.astype(jnp.bfloat16)


def solution(mesh):
    return jax.shard_map(
        shards,
        mesh=mesh,
        in_specs=(
            P("ctx", "tp"),
            P("ctx", "tp"),
            P("ctx", "tp"),
            P(None, None, "tp"),
            P("tp", None),
            P("tp", None),
            P("tp", None),
        ),
        out_specs=P("ctx", "tp"),
        check_vma=False,
    )
```

profile of v0, /device:TPU:1, one launch (start us, length us, event | category | flops | bytes accessed | tf_op | source)
XLA Modules:
  0.0 447.7 jit_solution(2728666328945808890)
XLA Ops:
  6.5 0.7 slice.92
  7.3 0.2 copy.47
  7.5 4.8 %collective-permute-start.1 = (bf16[2,512]{0,1:T(8,128)(2,1)S(1)}, bf16[2,512]{0,1:T(8,128)(2,1)S(1)}, u32[]{:S(2)}, u32[]{:S(2)}) collective-permute-start(bf16[2,512]{0,1:T(8,128)(2,1)S(1)} %copy.47), channel_id=1, source_target_pairs={{0,16},{16,32},{32,48},{48,64},{64,80},{80,96},{96,112},{112,128},... | collective-permute-start | bytes 6152 | tf_op jit(solution)/shard_map/ppermute | solution.py:12
  12.3 0.7 slice.99
  13.2 4.0 collective-permute-start.2
  17.2 0.9 fusion.57
  18.1 0.8 constant_dynamic-slice_fusion
  19.4 1.0 copy.48
  20.7 217.1 %gather_fusion = f32[65536,8]{1,0:T(8,128)} fusion(f32[8,256]{0,1:T(8,128)S(1)} %copy.54, s32[65536]{0:T(1024)S(1)} %broadcast_clamp_fusion), kind=kCustom, calls=%fused_computation | custom fusion | bytes 4456448 | tf_op jit(solution)/shard_map/while/body/eval_jaxpr/jit(_take)/gather | solution.py:50
  237.8 18.6 %copy.55 = f32[256,256,8]{1,0,2:T(8,128)S(1)} copy(f32[256,256,8]{2,1,0:T(8,128)} %bitcast.41) | data formatting | bytes 4194304 | tf_op jit(solution)/shard_map/while/body/eval_jaxpr/jit(_take)/gather | solution.py:50
  256.7 1.4 fusion.38
  258.1 18.1 %all-to-all-start = ((bf16[64,8,128]{2,1,0:T(8,128)(2,1)}), bf16[64,8,128]{2,1,0:T(8,128)(2,1)S(1)}, u32[]{:S(2)}, u32[]{:S(2)}) async-start(bf16[64,8,128]{2,1,0:T(8,128)(2,1)} %fusion.38), calls=%async_computation | async-start | bytes 262144 | tf_op jit(solution)/shard_map/all_to_all | solution.py:91
  276.3 13.9 %all-to-all-done = bf16[64,8,128]{2,1,0:T(8,128)(2,1)S(1)} async-done(((bf16[64,8,128]{2,1,0:T(8,128)(2,1)}), bf16[64,8,128]{2,1,0:T(8,128)(2,1)S(1)}, u32[]{:S(2)}, u32[]{:S(2)}) %all-to-all-start) | async-done | bytes 131104 | tf_op jit(solution)/shard_map/all_to_all | solution.py:91
  290.2 0.3 fusion.31
  290.5 0.9 fusion.1
  291.4 1.8 fusion.5
  293.2 0.5 fusion.9
  293.8 0.7 copy.56
  294.5 6.9 %all-to-all-start.1 = ((bf16[8,64,128]{2,0,1:T(8,128)(2,1)}), bf16[8,64,128]{2,0,1:T(8,128)(2,1)S(1)}, u32[]{:S(2)}, u32[]{:S(2)}) async-start(bf16[8,64,128]{2,0,1:T(8,128)(2,1)} %copy.56), calls=%async_computation.1 | async-start | bytes 262144 | tf_op jit(solution)/shard_map/all_to_all | solution.py:99
  301.7 2.9 collective-permute-start
  304.7 1.8 collective-permute-done
  306.7 8.8 %all-to-all-done.1 = bf16[8,64,128]{2,0,1:T(8,128)(2,1)S(1)} async-done(((bf16[8,64,128]{2,0,1:T(8,128)(2,1)}), bf16[8,64,128]{2,0,1:T(8,128)(2,1)S(1)}, u32[]{:S(2)}, u32[]{:S(2)}) %all-to-all-start.1) | async-done | bytes 131104 | tf_op jit(solution)/shard_map/all_to_all | solution.py:99
  315.5 4.1 fusion
  319.7 121.2 %reduce-scatter.2.cloned.1.call-done = bf16[256,128]{0,1:T(8,128)(2,1)} async-done(((bf16[4096,128]{0,1:T(8,128)(2,1)}), bf16[256,128]{0,1:T(8,128)(2,1)}) %reduce-scatter.2.cloned.1.call-update) | async-done | bytes 65552 | tf_op jit(solution)/shard_map/reduce_scatter | solution.py:102
  (32 shorter events, 1.9 us)
Async XLA Ops:
  6.5 13.9 %copy-start = (bf16[128,512]{1,0:T(8,128)(2,1)S(1)}, bf16[128,512]{1,0:T(8,128)(2,1)}, u32[]{:S(2)}) copy-start(bf16[128,512]{1,0:T(8,128)(2,1)} %param.9) | copy-start | bytes 393220
  7.5 248.9 %collective-permute-start.1 = (bf16[2,512]{0,1:T(8,128)(2,1)S(1)}, bf16[2,512]{0,1:T(8,128)(2,1)S(1)}, u32[]{:S(2)}, u32[]{:S(2)}) collective-permute-start(bf16[2,512]{0,1:T(8,128)(2,1)S(1)} %copy.47), channel_id=1, source_target_pairs={{0,16},{16,32},{32,48},{48,64},{64,80},{80,96},{96,112},{112,128},... | collective-permute-start | bytes 6152 | tf_op jit(solution)/shard_map/ppermute | solution.py:12
  13.2 243.3 %collective-permute-start.2 = (bf16[2,512]{0,1:T(8,128)(2,1)S(1)}, bf16[2,512]{0,1:T(8,128)(2,1)S(1)}, u32[]{:S(2)}, u32[]{:S(2)}) collective-permute-start(bf16[2,512]{0,1:T(8,128)(2,1)S(1)} %copy.49), channel_id=1, source_target_pairs={{0,16},{16,32},{32,48},{48,64},{64,80},{80,96},{96,112},{112,128},... | collective-permute-start | bytes 6152 | tf_op jit(solution)/shard_map/ppermute | solution.py:12
  258.1 32.1 %all-to-all-start = ((bf16[64,8,128]{2,1,0:T(8,128)(2,1)}), bf16[64,8,128]{2,1,0:T(8,128)(2,1)S(1)}, u32[]{:S(2)}, u32[]{:S(2)}) async-start(bf16[64,8,128]{2,1,0:T(8,128)(2,1)} %fusion.38), calls=%async_computation | async-start | bytes 262144 | tf_op jit(solution)/shard_map/all_to_all | solution.py:91
  291.4 10.1 %copy-start.1 = (bf16[128,512]{1,0:T(8,128)(2,1)S(1)}, bf16[128,512]{1,0:T(8,128)(2,1)}, u32[]{:S(2)}) copy-start(bf16[128,512]{1,0:T(8,128)(2,1)} %param.7) | copy-start | bytes 393220
  294.5 21.0 %all-to-all-start.1 = ((bf16[8,64,128]{2,0,1:T(8,128)(2,1)}), bf16[8,64,128]{2,0,1:T(8,128)(2,1)S(1)}, u32[]{:S(2)}, u32[]{:S(2)}) async-start(bf16[8,64,128]{2,0,1:T(8,128)(2,1)} %copy.56), calls=%async_computation.1 | async-start | bytes 262144 | tf_op jit(solution)/shard_map/all_to_all | solution.py:99
  301.4 139.5 %reduce-scatter.2.cloned.1.call-start = ((), (), s32[]{:S(2)}) async-start(), calls=%async_computation.3 | async-start | bytes 1114112 | tf_op jit(solution)/shard_map/reduce_scatter | solution.py:102
  301.7 4.9 %collective-permute-start = (bf16[2,512]{0,1:T(8,128)(2,1)S(1)}, bf16[2,512]{0,1:T(8,128)(2,1)S(1)}, u32[]{:S(2)}, u32[]{:S(2)}) collective-permute-start(bf16[2,512]{0,1:T(8,128)(2,1)S(1)} %copy.45), channel_id=1, source_target_pairs={{0,16},{16,32},{32,48},{48,64},{64,80},{80,96},{96,112},{112,128},... | collective-permute-start | bytes 6152 | tf_op jit(solution)/shard_map/ppermute | solution.py:12
Sparse Core Ops, SparseCore 0:
  319.8 121.0 reduce-scatter.1
where the time goes:
time: 448 us
  local copies, waits for them, and re-layouts  242 us (54%)
  waiting for transfers between devices  146 us (33%)
  starting transfers between devices  36.8 us (8%)
  between operations  13.7 us (3%)
  matrix products  7.61 us (2%)
    gather x2, local copies, waits for them, and re-layouts, modal_conv(): toeplitz = jnp.take(kernel, jnp.maximum(offset_table, 0), axis=1)  236 us
    reduce_scatter x1, waiting for transfers between devices, shards(): lax.psum_scatter(lax.dot_general(out_weight, gated, (((0,), (1,)), ((), (...  121 us
    all_to_all x1, starting transfers between devices, shards(): lax.all_to_all(product.T, 'ctx', split_axis=0, concat_axis=1, tiled=True)  18.1 us
    all_to_all x1, waiting for transfers between devices, shards(): lax.all_to_all(product.T, 'ctx', split_axis=0, concat_axis=1, tiled=True)  13.9 us
    ppermute x3, starting transfers between devices, shifted(): lax.ppermute(value, axis, [(source, source + steps) for source in range(i...  11.8 us
  transfers between devices with their start and end apart: 6, of which 4 were waited for; matrix products, arithmetic and copies ran while one was open for 54% of the time, Pallas kernels for 0%

commit v1 on v0

v1 whole, which is shorter than its diff:
```python
import jax
import jax.numpy as jnp
from jax import lax
from jax.experimental import pallas as pl
from jax.experimental.pallas import tpu as pltpu
from jax.sharding import PartitionSpec as P

MESH = pl.DeviceIdType.MESH
F32 = jnp.float32
BF16 = jnp.bfloat16
RUN = 8
BLOCK = 16
LANES = 128


def one_minus_exp(u):
    series = jnp.ones_like(u)
    for n in range(8, 1, -1):
        series = 1.0 - u * (1.0 / n) * series
    return jnp.where(u < 0.125, u * series, 1.0 - jnp.exp(-u))


def kernel(
    q_hbm, k_hbm, v_hbm, taps_hbm, rate_hbm, resid_hbm, w_hbm, o_ref,
    q_in, k_in, v_in, taps, rate_in, resid_in, w_own, w_par,
    q_ext, k_ext, v_ext, p_ext, p_group, halo_out, halo_in,
    rate, decay, coeff, heads, prefix, span, response, decay_b, gain_b, starts, local, q_feat,
    z_out, z_in, y_out, y_in, g_own, g_par, x_out, x_in, x_keep, h_out, h_in, unperm,
    in_sem, w_sem, wp_send, wp_recv, halo_sem, z_send, z_recv, y_send, y_recv, g_send, g_recv,
    x_send, x_recv, h_send, h_recv,
):
    rows, channels = q_in.shape
    rows_y, xs = y_in.shape[0] + 1, x_in.shape[1] + 1
    chunks, chunk = x_out.shape[0], x_out.shape[2]
    cols = h_out.shape[2]
    per = rows // BLOCK
    ctx, tp = lax.axis_index("ctx"), lax.axis_index("tp")
    y, z = ctx // RUN, ctx % RUN
    x, half, core = tp // 4, (tp // 2) % 2, tp % 2
    n_ctx = rows_y * RUN
    groups = [slice(g * LANES, (g + 1) * LANES) for g in range(channels // LANES)]

    def put(src, dst, send, recv, device):
        return pltpu.make_async_remote_copy(
            src_ref=src, dst_ref=dst, send_sem=send, recv_sem=recv, device_id=device, device_id_type=MESH
        )

    along_z = [(y * RUN + (z + d) % RUN, tp) for d in range(1, RUN)]
    along_y = [(((y + d) % rows_y) * RUN + z, tp) for d in range(1, rows_y)]
    along_x = [(ctx, ((x + d) % xs) * 4 + half * 2 + core) for d in range(1, xs)]
    other_core = (ctx, x * 4 + half * 2 + (1 - core))
    other_half = (ctx, x * 4 + (1 - half) * 2 + core)
    after, before = ((ctx + 1) % n_ctx, tp), ((ctx + n_ctx - 1) % n_ctx, tp)
    peers = along_z + along_y + along_x + [other_core, other_half, after, before]

    barrier = pltpu.get_barrier_semaphore()
    for peer in peers:
        pl.semaphore_signal(barrier, inc=1, device_id=peer, device_id_type=MESH)

    loads = [
        pltpu.make_async_copy(src, dst, in_sem.at[i])
        for i, (src, dst) in enumerate(
            [(q_hbm, q_in), (k_hbm, k_in), (v_hbm, v_in), (taps_hbm, taps), (rate_hbm, rate_in), (resid_hbm, resid_in)]
        )
    ]
    for load in loads:
        load.start()
    blocks = 2 * xs
    w_loads = [
        pltpu.make_async_copy(
            w_hbm.at[:, pl.ds(pl.multiple_of(b * 2 * cols + core * cols, cols), cols)], w_own.at[b], w_sem.at[b]
        )
        for b in range(blocks)
    ]
    w_shares = [
        put(
            w_hbm.at[:, pl.ds(pl.multiple_of(b * 2 * cols + (1 - core) * cols, cols), cols)],
            w_par.at[b], wp_send.at[b], wp_recv.at[b], other_core,
        )
        for b in range(blocks)
    ]

    for load in loads:
        load.wait()
    halo_out[...] = jnp.zeros((8, channels), F32)
    for s, stream in enumerate([q_in, k_in, v_in]):
        last = stream[rows - 16 :, :].astype(F32)
        halo_out[2 * s : 2 * s + 2, :] = last[14:16]
    for ext in (k_ext, v_ext):
        ext[0:8, :] = jnp.zeros((8, channels), F32)
    pl.semaphore_wait(barrier, len(peers))
    halo = put(halo_out, halo_in, halo_sem.at[0], halo_sem.at[1], after)
    halo.start()
    for w_load in w_loads:
        w_load.start()

    for stream, ext in [(k_in, k_ext), (v_in, v_ext)]:
        for a in range(0, rows, 16):
            ext[8 + a : 24 + a, :] = stream[a : a + 16, :].astype(F32)

    def feature(ext, n, first, count):
        total = taps[n, 0:1, :] * ext[8 + first : 8 + first + count, :]
        total = total + taps[n, 1:2, :] * ext[7 + first : 7 + first + count, :]
        return total + taps[n, 2:3, :] * ext[6 + first : 6 + first + count, :]

    def product(first, count):
        value = feature(k_ext, 1, first, count) * feature(v_ext, 2, first, count)
        return value.astype(BF16).astype(F32)

    row_index = lax.broadcasted_iota(jnp.int32, (8, channels), 0)
    p_ext[0:8, :] = jnp.where(row_index < 2, 0.0, product(0, 8))
    for a in range(8, rows, 8):
        p_ext[a : a + 8, :] = product(a, 8)

    rate[...] = rate_in[...]
    decay[...] = jnp.exp(-rate[...])
    coeff[...] = resid_in[...] * jnp.sqrt(one_minus_exp(2.0 * rate[...]))

    step = decay[...]
    low, high = jnp.zeros_like(step), jnp.zeros_like(step)
    for t in range(rows // 2):
        if t % BLOCK == 0:
            prefix[t // BLOCK] = low
            prefix[(t + rows // 2) // BLOCK] = high
        low = step * low + p_ext[t : t + 1, :]
        high = step * high + p_ext[t + rows // 2 : t + rows // 2 + 1, :]
    middle, modes = low, step.shape[0]
    own = high + jnp.exp(rate[...] * (-0.5 * rows)) * middle
    head_gain = jnp.exp(rate[...] * (2.0 - rows))
    whole = jnp.exp(rate[...] * (-1.0 * rows))

    halo.wait()
    inside = jnp.where(ctx > 0, halo_in[...], 0.0)
    k_ext[6:8, :] = inside[2:4, :]
    v_ext[6:8, :] = inside[4:6, :]
    p_ext[0:8, :] = product(0, 8)
    heads[...] = step * p_ext[0:1, :] + p_ext[1:2, :]
    own = own + head_gain * heads[...]

    z_out[...] = own.astype(BF16)
    z_copies = [put(z_out, z_in.at[d - 1], z_send.at[d - 1], z_recv.at[d - 1], along_z[d - 1]) for d in range(1, RUN)]
    for copy in z_copies:
        copy.start()
    for w_share in w_shares:
        w_share.start()

    for b in range(1, per):
        span[b] = jnp.exp(rate[...] * (2.0 - BLOCK * b))
        if b > per // 2:
            prefix[b] = prefix[b] + jnp.exp(rate[...] * (1.0 * (per // 2 - b) * BLOCK)) * middle
    prefix[per // 2] = middle
    term = coeff[...]
    for k in range(BLOCK):
        response[k : k + 1, :] = jnp.sum(term, axis=0, keepdims=True)
        term = term * step
    first_gain = coeff[...] * step
    for g, lanes in enumerate(groups):
        for b in range(per):
            decay_b[g, pl.ds(b, modes, stride=per), :] = step[:, lanes]
            gain_b[g, pl.ds(b, modes, stride=per), :] = first_gain[:, lanes]
        q_ext[g, 6:8, :] = inside[0:2, lanes]
        for a in range(0, rows, 16):
            q_ext[g, 8 + a : 24 + a, :] = q_in[a : a + 16, lanes].astype(F32)
            p_group[g, a : a + 16, :] = p_ext[a : a + 16, lanes]
        for r in range(BLOCK):
            total = taps[0, 0:1, lanes] * q_ext[g, pl.ds(8 + r, per, stride=BLOCK), :]
            total = total + taps[0, 1:2, lanes] * q_ext[g, pl.ds(7 + r, per, stride=BLOCK), :]
            total = total + taps[0, 2:3, lanes] * q_ext[g, pl.ds(6 + r, per, stride=BLOCK), :]
            q_feat[r * per : (r + 1) * per, lanes] = total

    def convolve(group, carry):
        lanes = pl.ds(pl.multiple_of(group * LANES, LANES), LANES)
        inputs = [p_group[group, pl.ds(r, per, stride=BLOCK), :] for r in range(BLOCK)]
        for r in range(BLOCK):
            total = response[0:1, lanes] * inputs[r]
            for k in range(1, r + 1):
                total = total + response[k : k + 1, lanes] * inputs[r - k]
            local[r * per : (r + 1) * per, lanes] = total
        return carry

    lax.fori_loop(0, channels // LANES, convolve, 0)

    for copy in z_copies:
        copy.wait()
    before_me = jnp.zeros_like(step)
    for d in range(RUN - 1, 0, -1):
        before_me = whole * before_me + jnp.where(d <= z, z_in[d - 1].astype(F32), 0.0)
    total = whole * before_me + own
    for d in range(RUN - 1, 0, -1):
        total = jnp.where(d > z, whole * total + z_in[d - 1].astype(F32), total)

    y_out[...] = total.astype(BF16)
    y_copies = [
        put(y_out, y_in.at[d - 1], y_send.at[d - 1], y_recv.at[d - 1], along_y[d - 1]) for d in range(1, rows_y)
    ]
    for copy in y_copies:
        copy.start()
    row_decay = jnp.exp(rate[...] * (-1.0 * rows * RUN))
    my_decay = jnp.exp(rate[...] * (-1.0 * rows * z.astype(F32)))
    for w_load in w_loads:
        w_load.wait()
    for w_share in w_shares:
        w_share.wait()
    for copy in y_copies:
        copy.wait()
    arriving = jnp.zeros_like(step)
    for d in range(rows_y - 1, 0, -1):
        arriving = row_decay * arriving + jnp.where(d <= y, y_in[d - 1].astype(F32), 0.0)
    state = before_me + my_decay * arriving
    second = step * step * state + heads[...]
    for b in range(per):
        if b > 0:
            state = prefix[b] + span[b] * second
        for g, lanes in enumerate(groups):
            starts[g, pl.ds(b, modes, stride=per), :] = state[:, lanes]

    steps = BLOCK // chunks
    g_copies, x_copies, h_copies = [], [], []
    for c in range(chunks):

        def gate(group, carry):
            lanes = pl.ds(pl.multiple_of(group * LANES, LANES), LANES)
            shape = (modes, per, LANES)
            ratio = decay_b[group].reshape(shape)
            term = starts[group].reshape(shape)
            if c == 0:
                term = term * gain_b[group].reshape(shape)
            for r in range(c * steps, (c + 1) * steps, 2):
                pair = []
                for one in (r, r + 1):
                    here = slice(one * per, (one + 1) * per)
                    value = local[here, lanes] + jnp.sum(term, axis=0)
                    term = term * ratio
                    pair.append(q_feat[here, lanes] * value.astype(BF16).astype(F32))
                g_own[r * per : (r + 2) * per, lanes] = jnp.concatenate(pair, axis=0).astype(BF16)
            if c + 1 < chunks:
                starts[group] = term.reshape(modes * per, LANES)
            return carry

        lax.fori_loop(0, channels // LANES, gate, 0)
        piece = pl.ds(c * chunk, chunk)
        copy = put(g_own.at[piece], g_par.at[piece], g_send.at[c], g_recv.at[c], other_core)
        copy.start()
        g_copies.append(copy)

    for c in range(chunks):
        g_copies[c].wait()
        here = slice(c * chunk, (c + 1) * chunk)
        mine, theirs = g_own[here, :], g_par[here, :]

        def share(b):
            return jnp.dot(mine, w_own[b], preferred_element_type=F32) + jnp.dot(
                theirs, w_par[b], preferred_element_type=F32
            )

        for d in (2, 1, 3):
            to = (x + d) % xs
            for h in range(2):
                x_out[c, d - 1, :, h * cols : (h + 1) * cols] = share(to * 2 + h).astype(BF16)
            copy = put(x_out.at[c, d - 1], x_in.at[c, d - 1], x_send.at[c, d - 1], x_recv.at[c, d - 1], along_x[d - 1])
            copy.start()
            x_copies.append(copy)
        for h in range(2):
            x_keep[c, h] = share(x * 2 + h)

    for c in range(chunks):
        for copy in x_copies[c * (xs - 1) : (c + 1) * (xs - 1)]:
            copy.wait()
        for h in range(2):
            for a in range(0, chunk, 16):
                value = x_keep[c, h, a : a + 16, :]
                for d in range(1, xs):
                    value = value + x_in[c, d - 1, a : a + 16, h * cols : (h + 1) * cols].astype(F32)
                x_keep[c, h, a : a + 16, :] = value
        h_out[c] = x_keep[c, 1 - half].astype(BF16)
        copy = put(h_out.at[c], h_in.at[c], h_send.at[c], h_recv.at[c], other_half)
        copy.start()
        h_copies.append(copy)

    for c in range(chunks):
        h_copies[c].wait()
        for a in range(0, chunk, 16):
            value = x_keep[c, half, a : a + 16, :] + h_in[c, a : a + 16, :].astype(F32)
            r = (c * chunk + a) // per
            for i in range(16 // per):
                for g in range(cols // LANES):
                    part = value[i * per : (i + 1) * per, g * LANES : (g + 1) * LANES]
                    unperm[g, pl.ds(r + i, per, stride=BLOCK), :] = part
    for g in range(cols // LANES):
        o_ref[:, g * LANES : (g + 1) * LANES] = unperm[g].astype(BF16)


def solution(mesh):
    n_ctx, n_tp = mesh.shape["ctx"], mesh.shape["tp"]
    rows_y, xs = n_ctx // RUN, n_tp // 4
    chunks = 2

    def shards(queries, keys, values, short_taps, long_rates, long_resid, out_weight):
        rows, channels = queries.shape
        modes = long_rates.shape[1]
        out = out_weight.shape[1]
        cols = out // n_tp
        chunk = rows // chunks
        state = (modes, channels)
        stream = pltpu.VMEM((rows, channels), BF16)
        sem = pltpu.SemaphoreType.DMA
        return pl.pallas_call(
            kernel,
            name="hyena",
            out_shape=jax.ShapeDtypeStruct((rows, cols), BF16),
            in_specs=[pl.BlockSpec(memory_space=pltpu.HBM)] * 7,
            out_specs=pl.BlockSpec(memory_space=pltpu.VMEM),
            scratch_shapes=[
                stream, stream, stream,
                pltpu.VMEM(short_taps.shape, F32),
                pltpu.VMEM(state, F32),
                pltpu.VMEM(state, F32),
                pltpu.VMEM((2 * xs, channels, cols), BF16),
                pltpu.VMEM((2 * xs, channels, cols), BF16),
                pltpu.VMEM((channels // LANES, rows + 8, LANES), F32),
                pltpu.VMEM((rows + 8, channels), F32),
                pltpu.VMEM((rows + 8, channels), F32),
                pltpu.VMEM((rows, channels), F32),
                pltpu.VMEM((channels // LANES, rows, LANES), F32),
                pltpu.VMEM((8, channels), F32),
                pltpu.VMEM((8, channels), F32),
                pltpu.VMEM(state, F32),
                pltpu.VMEM(state, F32),
                pltpu.VMEM(state, F32),
                pltpu.VMEM(state, F32),
                pltpu.VMEM((rows // BLOCK,) + state, F32),
                pltpu.VMEM((rows // BLOCK,) + state, F32),
                pltpu.VMEM((BLOCK, channels), F32),
                pltpu.VMEM((channels // LANES, modes * (rows // BLOCK), LANES), F32),
                pltpu.VMEM((channels // LANES, modes * (rows // BLOCK), LANES), F32),
                pltpu.VMEM((channels // LANES, modes * (rows // BLOCK), LANES), F32),
                pltpu.VMEM((rows, channels), F32),
                pltpu.VMEM((rows, channels), F32),
                pltpu.VMEM(state, BF16),
                pltpu.VMEM((RUN - 1,) + state, BF16),
                pltpu.VMEM(state, BF16),
                pltpu.VMEM((rows_y - 1,) + state, BF16),
                stream, stream,
                pltpu.VMEM((chunks, xs - 1, chunk, 2 * cols), BF16),
                pltpu.VMEM((chunks, xs - 1, chunk, 2 * cols), BF16),
                pltpu.VMEM((chunks, 2, chunk, cols), F32),
                pltpu.VMEM((chunks, chunk, cols), BF16),
                pltpu.VMEM((chunks, chunk, cols), BF16),
                pltpu.VMEM((cols // LANES, rows, LANES), F32),
                sem((6,)),
                sem((2 * xs,)), sem((2 * xs,)), sem((2 * xs,)),
                sem((2,)),
                sem((RUN - 1,)), sem((RUN - 1,)),
                sem((rows_y - 1,)), sem((rows_y - 1,)),
                sem((chunks,)), sem((chunks,)),
                sem((chunks, xs - 1)), sem((chunks, xs - 1)),
                sem((chunks,)), sem((chunks,)),
            ],
            compiler_params=pltpu.CompilerParams(
                collective_id=0, has_side_effects=True, vmem_limit_bytes=62 * 1024 * 1024
            ),
        )(queries, keys, values, short_taps, long_rates.T, long_resid.T, out_weight)

    return jax.shard_map(
        shards,
        mesh=mesh,
        in_specs=(
            P("ctx", "tp"),
            P("ctx", "tp"),
            P("ctx", "tp"),
            P(None, None, "tp"),
            P("tp", None),
            P("tp", None),
            P("tp", None),
        ),
        out_specs=P("ctx", "tp"),
        check_vma=False,
    )
```

time: 448 us -> 58.5 us (0.13)
  local copies, waits for them, and re-layouts: 242 us -> 1.47 us
  waiting for transfers between devices: 146 us -> 0 us
  Pallas kernels: 0 us -> 56.8 us
  starting transfers between devices: 36.8 us -> 0 us
  between operations: 13.7 us -> 0.01 us
  matrix products: 7.61 us -> 0 us
    gather x2 -> x0, local copies, waits for them, and re-layouts: 236 us -> none  [modal_conv(): toeplitz = jnp.take(kernel, jnp.maximum(offset_table, 0), axis=1)]
    reduce_scatter x1 -> x0, waiting for transfers between devices: 121 us -> none  [shards(): lax.psum_scatter(lax.dot_general(out_weight, gated, (((0,), (1,)), ((), (...]
    pallas_call x0 -> x1, Pallas kernels: none -> 56.8 us  [shards(): pl.pallas_call(kernel, name='hyena', out_shape=jax.ShapeDtypeStruct((rows...]
    all_to_all x2 -> x0, starting transfers between devices: 25 us -> none  [the longest x1 18.1 us: shards(): lax.all_to_all(product.T, 'ctx', split_axis=0, concat_axis=1, tiled=True)]
    all_to_all x2 -> x0, waiting for transfers between devices: 22.7 us -> none  [the longest x1 13.9 us: shards(): lax.all_to_all(product.T, 'ctx', split_axis=0, concat_axis=1, tiled=True)]
    ppermute x3 -> x0, starting transfers between devices: 11.8 us -> none  [shifted(): lax.ppermute(value, axis, [(source, source + steps) for source in range(i...]
    dot_general x5 -> x0, matrix products: 7.61 us -> none  [the longest x1 4.14 us: shards(): lax.dot_general(out_weight, gated, (((0,), (1,)), ((), ())), preferred_el...]
  transfers between devices with their start and end apart: 6 -> 0, of which waited for: 4 -> 0; matrix products, arithmetic and copies ran while one was open for 54% -> 0% of each run, Pallas kernels for 0% -> 0%
where the time goes in v1:
time: 58.5 us; the launch traced here: 58.3 us
  Pallas kernels  56.8 us (97%)
  local copies, waits for them, and re-layouts  1.47 us (3%)
    pallas_call x1, Pallas kernels, shards(): pl.pallas_call(kernel, name='hyena', out_shape=jax.ShapeDtypeStruct((rows...  56.8 us
    unnamed x1, local copies, waits for them, and re-layouts  1.47 us

profile of v1, /device:TPU:1, one launch (start us, length us, event | category | flops | bytes accessed | tf_op | source)
XLA Modules:
  0.0 58.3 jit_solution(1408174829479986515)
XLA Ops:
  0.0 56.8 %hyena.1 = bf16[128,256]{1,0:T(8,128)(2,1)} custom-call(bf16[128,512]{1,0:T(8,128)(2,1)} %q_hbm.1, bf16[128,512]{1,0:T(8,128)(2,1)} %k_hbm.1, bf16[128,512]{1,0:T(8,128)(2,1)} %v_hbm.1, f32[3,3,512]{2,1,0:T(4,128)} %taps_hbm.1, f32[16,512]{1,0:T(8,128)} %bitcast.2, f32[16,512]{1,0:T(8,128)} %bitcast.3, bf16[512,4096]{1,0:T(8,128)(2,1)} %w_hbm.1), custom_call_target="tpu_custom_call" | custom-call | tf_op jit(solution)/shard_map/hyena/pallas_call | solution.py:307
  56.8 1.5 %copy.9 = bf16[128,256]{1,0:T(8,128)(2,1)} copy(bf16[128,256]{1,0:T(8,128)(2,1)} %hyena.1) | data formatting | bytes 131072

commit v2 on v1

--- a/solution.py
+++ b/solution.py
@@ -18,6 +18,17 @@
     for n in range(8, 1, -1):
         series = 1.0 - u * (1.0 / n) * series
     return jnp.where(u < 0.125, u * series, 1.0 - jnp.exp(-u))
+
+
+def packed(parts):
+    value = jnp.concatenate(parts, axis=0)
+    width = value.shape[1] // 2
+    return jnp.concatenate([value[:, :width], value[:, width:]], axis=0).astype(BF16)
+
+
+def unpacked(block):
+    value = block.astype(F32)
+    return jnp.concatenate([value[0:8], value[8:16]], axis=1)
 
 
 def kernel(
@@ -27,11 +38,11 @@
     rate, decay, coeff, heads, prefix, span, response, decay_b, gain_b, starts, local, q_feat,
     z_out, z_in, y_out, y_in, g_own, g_par, x_out, x_in, x_keep, h_out, h_in, unperm,
     in_sem, w_sem, wp_send, wp_recv, halo_sem, z_send, z_recv, y_send, y_recv, g_send, g_recv,
-    x_send, x_recv, h_send, h_recv,
+    x_send, x_recv, h_send, h_recv, ring_sem,
 ):
     rows, channels = q_in.shape
-    rows_y, xs = y_in.shape[0] + 1, x_in.shape[1] + 1
-    chunks, chunk = x_out.shape[0], x_out.shape[2]
+    rows_y, xs = y_in.shape[0], x_in.shape[2] + 1
+    chunks, chunk = h_out.shape[0], h_out.shape[1]
     cols = h_out.shape[2]
     per = rows // BLOCK
     ctx, tp = lax.axis_index("ctx"), lax.axis_index("tp")
@@ -51,10 +62,14 @@
     other_core = (ctx, x * 4 + half * 2 + (1 - core))
     other_half = (ctx, x * 4 + (1 - half) * 2 + core)
     after, before = ((ctx + 1) % n_ctx, tp), ((ctx + n_ctx - 1) % n_ctx, tp)
-    peers = along_z + along_y + along_x + [other_core, other_half, after, before]
+
+    far_mate = (y * RUN + (z + RUN // 2) % RUN, other_half[1])
+    near_y = [d for d in range(1, rows_y) if min(d, rows_y - d) <= 2]
+    hop_y = [d for d in range(1, rows_y) if min(d, rows_y - d) == 2]
+    told = along_z + along_x + [other_core, before, far_mate] + [along_y[d - 1] for d in near_y]
 
     barrier = pltpu.get_barrier_semaphore()
-    for peer in peers:
+    for peer in told:
         pl.semaphore_signal(barrier, inc=1, device_id=peer, device_id_type=MESH)
 
     loads = [
@@ -82,17 +97,10 @@
 
     for load in loads:
         load.wait()
-    halo_out[...] = jnp.zeros((8, channels), F32)
-    for s, stream in enumerate([q_in, k_in, v_in]):
-        last = stream[rows - 16 :, :].astype(F32)
-        halo_out[2 * s : 2 * s + 2, :] = last[14:16]
+    for w_load in w_loads:
+        w_load.start()
     for ext in (k_ext, v_ext):
         ext[0:8, :] = jnp.zeros((8, channels), F32)
-    pl.semaphore_wait(barrier, len(peers))
-    halo = put(halo_out, halo_in, halo_sem.at[0], halo_sem.at[1], after)
-    halo.start()
-    for w_load in w_loads:
-        w_load.start()
 
     for stream, ext in [(k_in, k_ext), (v_in, v_ext)]:
         for a in range(0, rows, 16):
@@ -129,20 +137,39 @@
     head_gain = jnp.exp(rate[...] * (2.0 - rows))
     whole = jnp.exp(rate[...] * (-1.0 * rows))
 
+    k_first, v_first = k_in[0:16, :].astype(F32), v_in[0:16, :].astype(F32)
+    q_last, k_last, v_last = (stream[rows - 16 :, :].astype(F32)[14:16] for stream in (q_in, k_in, v_in))
+    z_out[:, :channels] = own.astype(BF16)
+    z_out[:, channels:] = packed([k_first[0:2], v_first[0:2], k_last, v_last])
+    z_in[z] = z_out[...]
+    halo_out[...] = packed([q_last, k_last, v_last, jnp.zeros_like(v_last)])
+    pl.semaphore_wait(barrier, len(told))
+    z_copies = [put(z_out, z_in.at[z], z_send.at[d - 1], z_recv.at[z], along_z[d - 1]) for d in range(1, RUN)]
+    for copy in z_copies:
+        copy.start()
+    for d in hop_y:
+        pl.semaphore_signal(ring_sem, inc=1, device_id=along_y[d - 1], device_id_type=MESH)
+    halo = put(halo_out, halo_in, halo_sem.at[0], halo_sem.at[1], after)
+    halo.start()
+    for w_share in w_shares:
+        w_share.start()
+
     halo.wait()
-    inside = jnp.where(ctx > 0, halo_in[...], 0.0)
+    inside = jnp.where(ctx > 0, unpacked(halo_in[...]), 0.0)
     k_ext[6:8, :] = inside[2:4, :]
     v_ext[6:8, :] = inside[4:6, :]
     p_ext[0:8, :] = product(0, 8)
     heads[...] = step * p_ext[0:1, :] + p_ext[1:2, :]
-    own = own + head_gain * heads[...]
-
-    z_out[...] = own.astype(BF16)
-    z_copies = [put(z_out, z_in.at[d - 1], z_send.at[d - 1], z_recv.at[d - 1], along_z[d - 1]) for d in range(1, RUN)]
-    for copy in z_copies:
-        copy.start()
-    for w_share in w_shares:
-        w_share.start()
+
+    def boundary(last, first):
+        value = [1.0, 1.0]
+        for n, old, new in ((1, 4, 0), (2, 6, 2)):
+            tap = [taps[n, j : j + 1, :] for j in range(3)]
+            line = [last[old : old + 1], last[old + 1 : old + 2], first[new : new + 1], first[new + 1 : new + 2]]
+            for i in range(2):
+                value[i] = value[i] * (tap[0] * line[i + 2] + tap[1] * line[i + 1] + tap[2] * line[i])
+        value = [one.astype(BF16).astype(F32) for one in value]
+        return step * value[0] + value[1]
 
     for b in range(1, per):
         span[b] = jnp.exp(rate[...] * (2.0 - BLOCK * b))
@@ -180,33 +207,50 @@
 
     lax.fori_loop(0, channels // LANES, convolve, 0)
 
-    for copy in z_copies:
-        copy.wait()
-    before_me = jnp.zeros_like(step)
-    for d in range(RUN - 1, 0, -1):
-        before_me = whole * before_me + jnp.where(d <= z, z_in[d - 1].astype(F32), 0.0)
-    total = whole * before_me + own
-    for d in range(RUN - 1, 0, -1):
-        total = jnp.where(d > z, whole * total + z_in[d - 1].astype(F32), total)
-
-    y_out[...] = total.astype(BF16)
-    y_copies = [
-        put(y_out, y_in.at[d - 1], y_send.at[d - 1], y_recv.at[d - 1], along_y[d - 1]) for d in range(1, rows_y)
-    ]
-    for copy in y_copies:
-        copy.start()
+    for d in range(1, RUN):
+        z_copies[d - 1].wait_send()
+        there = (z + d) % RUN
+        put(z_out, z_in.at[there], z_send.at[d - 1], z_recv.at[there], along_z[d - 1]).wait_recv()
+    before_me, total = jnp.zeros_like(step), jnp.zeros_like(step)
+    edges = [unpacked(z_in[i, :, channels:]) for i in range(RUN)]
+    for i in range(RUN):
+        value = z_in[i, :, :channels].astype(F32)
+        if i > 0:
+            value = value + head_gain * boundary(edges[i - 1], edges[i])
+        before_me = jnp.where(i < z, whole * before_me + value, before_me)
+        total = whole * total + value
+
+    y_out[:, :channels] = total.astype(BF16)
+    row_edges = [edges[0][0:2], edges[0][2:4], edges[RUN - 1][4:6], edges[RUN - 1][6:8]]
+    y_out[:, channels:] = packed(row_edges)
+    y_in[y] = y_out[...]
+    pl.semaphore_wait(ring_sem, len(hop_y))
+    y_copies = [put(y_out, y_in.at[y], y_send.at[d - 1], y_recv.at[y], along_y[d - 1]) for d in range(1, rows_y)]
+    for d in sorted(range(1, rows_y), key=lambda d: -min(d, rows_y - d)):
+        pl.when(y + d < rows_y)(y_copies[d - 1].start)
     row_decay = jnp.exp(rate[...] * (-1.0 * rows * RUN))
-    my_decay = jnp.exp(rate[...] * (-1.0 * rows * z.astype(F32)))
+    row_gain = jnp.exp(rate[...] * (2.0 - rows * RUN))
+    my_gain = jnp.exp(rate[...] * (2.0 - rows * z.astype(F32)))
     for w_load in w_loads:
         w_load.wait()
     for w_share in w_shares:
         w_share.wait()
-    for copy in y_copies:
-        copy.wait()
-    arriving = jnp.zeros_like(step)
-    for d in range(rows_y - 1, 0, -1):
-        arriving = row_decay * arriving + jnp.where(d <= y, y_in[d - 1].astype(F32), 0.0)
-    state = before_me + my_decay * arriving
+    for d in range(1, rows_y):
+        pl.when(y + d < rows_y)(y_copies[d - 1].wait_send)
+        there = (y + rows_y - d) % rows_y
+        arrived = put(y_out, y_in.at[there], y_send.at[d - 1], y_recv.at[there], along_y[d - 1])
+        pl.when(y >= d)(arrived.wait_recv)
+    state = jnp.zeros_like(step)
+    last = jnp.zeros((8, channels), F32)
+    row_heads = jnp.zeros_like(step)
+    for i in range(rows_y):
+        edge = unpacked(y_in[i, :, channels:])
+        head = boundary(last, edge)
+        row_heads = jnp.where(i == y, head, row_heads)
+        value = row_decay * state + row_gain * head + y_in[i, :, :channels].astype(F32)
+        state = jnp.where(i < y, value, state)
+        last = edge
+    state = jnp.where(z > 0, before_me + my_gain * (step * step * state + row_heads), state)
     second = step * step * state + heads[...]
     for b in range(per):
         if b > 0:
@@ -243,44 +287,50 @@
         copy.start()
         g_copies.append(copy)
 
-    for c in range(chunks):
-        g_copies[c].wait()
+    def share(c, b):
         here = slice(c * chunk, (c + 1) * chunk)
-        mine, theirs = g_own[here, :], g_par[here, :]
-
-        def share(b):
-            return jnp.dot(mine, w_own[b], preferred_element_type=F32) + jnp.dot(
-                theirs, w_par[b], preferred_element_type=F32
-            )
-
-        for d in (2, 1, 3):
-            to = (x + d) % xs
-            for h in range(2):
-                x_out[c, d - 1, :, h * cols : (h + 1) * cols] = share(to * 2 + h).astype(BF16)
-            copy = put(x_out.at[c, d - 1], x_in.at[c, d - 1], x_send.at[c, d - 1], x_recv.at[c, d - 1], along_x[d - 1])
-            copy.start()
-            x_copies.append(copy)
-        for h in range(2):
-            x_keep[c, h] = share(x * 2 + h)
-
-    for c in range(chunks):
-        for copy in x_copies[c * (xs - 1) : (c + 1) * (xs - 1)]:
-            copy.wait()
-        for h in range(2):
+        value = jnp.dot(g_own[here, :], w_own[b], preferred_element_type=F32)
+        return value + jnp.dot(g_par[here, :], w_par[b], preferred_element_type=F32)
+
+    for part, h in enumerate((1 - half, half)):
+        for c in range(chunks):
+            if part == 0:
+                g_copies[c].wait()
+            for d in (2, 1, 3):
+                to = (x + d) % xs
+                x_out[part, c, d - 1] = share(c, to * 2 + h).astype(BF16)
+                copy = put(
+                    x_out.at[part, c, d - 1], x_in.at[part, c, d - 1],
+                    x_send.at[part, c, d - 1], x_recv.at[part, c, d - 1], along_x[d - 1],
+                )
+                copy.start()
+                x_copies.append(copy)
+    for part, h in enumerate((1 - half, half)):
+        for c in range(chunks):
+            x_keep[part, c] = share(c, x * 2 + h)
+
+    for part in range(2):
+        for c in range(chunks):
+            for copy in x_copies[: xs - 1]:
+                copy.wait()
+            x_copies = x_copies[xs - 1 :]
             for a in range(0, chunk, 16):
-                value = x_keep[c, h, a : a + 16, :]
+                value = x_keep[part, c, a : a + 16, :]
                 for d in range(1, xs):
-                    value = value + x_in[c, d - 1, a : a + 16, h * cols : (h + 1) * cols].astype(F32)
-                x_keep[c, h, a : a + 16, :] = value
-        h_out[c] = x_keep[c, 1 - half].astype(BF16)
-        copy = put(h_out.at[c], h_in.at[c], h_send.at[c], h_recv.at[c], other_half)
-        copy.start()
-        h_copies.append(copy)
+                    value = value + x_in[part, c, d - 1, a : a + 16, :].astype(F32)
+                if part == 0:
+                    h_out[c, a : a + 16, :] = value.astype(BF16)
+                else:
+                    x_keep[part, c, a : a + 16, :] = value
+            if part == 0:
+                copy = put(h_out.at[c], h_in.at[c], h_send.at[c], h_recv.at[c], other_half)
+                copy.start()
+                h_copies.append(copy)
 
     for c in range(chunks):
         h_copies[c].wait()
         for a in range(0, chunk, 16):
-            value = x_keep[c, half, a : a + 16, :] + h_in[c, a : a + 16, :].astype(F32)
+            value = x_keep[1, c, a : a + 16, :] + h_in[c, a : a + 16, :].astype(F32)
             r = (c * chunk + a) // per
             for i in range(16 // per):
                 for g in range(cols // LANES):
@@ -302,12 +352,13 @@
         cols = out // n_tp
         chunk = rows // chunks
         state = (modes, channels)
+        message = (modes, channels + channels // 2)
         stream = pltpu.VMEM((rows, channels), BF16)
         sem = pltpu.SemaphoreType.DMA
         return pl.pallas_call(
             kernel,
             name="hyena",
-            out_shape=jax.ShapeDtypeStruct((rows, cols), BF16),
+            out_shape=pltpu.VMEM((rows, cols), BF16),
             in_specs=[pl.BlockSpec(memory_space=pltpu.HBM)] * 7,
             out_specs=pl.BlockSpec(memory_space=pltpu.VMEM),
             scratch_shapes=[
@@ -322,8 +373,8 @@
                 pltpu.VMEM((rows + 8, channels), F32),
                 pltpu.VMEM((rows, channels), F32),
                 pltpu.VMEM((channels // LANES, rows, LANES), F32),
-                pltpu.VMEM((8, channels), F32),
-                pltpu.VMEM((8, channels), F32),
+                pltpu.VMEM((16, channels // 2), BF16),
+                pltpu.VMEM((16, channels // 2), BF16),
                 pltpu.VMEM(state, F32),
                 pltpu.VMEM(state, F32),
                 pltpu.VMEM(state, F32),
@@ -336,25 +387,26 @@
                 pltpu.VMEM((channels // LANES, modes * (rows // BLOCK), LANES), F32),
                 pltpu.VMEM((rows, channels), F32),
                 pltpu.VMEM((rows, channels), F32),
-                pltpu.VMEM(state, BF16),
-                pltpu.VMEM((RUN - 1,) + state, BF16),
-                pltpu.VMEM(state, BF16),
-                pltpu.VMEM((rows_y - 1,) + state, BF16),
+                pltpu.VMEM(message, BF16),
+                pltpu.VMEM((RUN,) + message, BF16),
+                pltpu.VMEM(message, BF16),
+                pltpu.VMEM((rows_y,) + message, BF16),
                 stream, stream,
-                pltpu.VMEM((chunks, xs - 1, chunk, 2 * cols), BF16),
-                pltpu.VMEM((chunks, xs - 1, chunk, 2 * cols), BF16),
-                pltpu.VMEM((chunks, 2, chunk, cols), F32),
+                pltpu.VMEM((2, chunks, xs - 1, chunk, cols), BF16),
+                pltpu.VMEM((2, chunks, xs - 1, chunk, cols), BF16),
+                pltpu.VMEM((2, chunks, chunk, cols), F32),
                 pltpu.VMEM((chunks, chunk, cols), BF16),
                 pltpu.VMEM((chunks, chunk, cols), BF16),
                 pltpu.VMEM((cols // LANES, rows, LANES), F32),
                 sem((6,)),
                 sem((2 * xs,)), sem((2 * xs,)), sem((2 * xs,)),
                 sem((2,)),
-                sem((RUN - 1,)), sem((RUN - 1,)),
-                sem((rows_y - 1,)), sem((rows_y - 1,)),
+                sem((RUN - 1,)), sem((RUN,)),
+                sem((rows_y - 1,)), sem((rows_y,)),
                 sem((chunks,)), sem((chunks,)),
-                sem((chunks, xs - 1)), sem((chunks, xs - 1)),
+                sem((2, chunks, xs - 1)), sem((2, chunks, xs - 1)),
                 sem((chunks,)), sem((chunks,)),
+                pltpu.SemaphoreType.REGULAR,
             ],
             compiler_params=pltpu.CompilerParams(
                 collective_id=0, has_side_effects=True, vmem_limit_bytes=62 * 1024 * 1024

time: 58.5 us -> 54.9 us (0.938)
  the two profiles are of different devices: /device:TPU:1 before, /device:TPU:9 now
where the time goes in v2:
time: 54.9 us; the launch traced here: 54.8 us
  Pallas kernels  54.1 us (99%)
  local copies, waits for them, and re-layouts  0.63 us (1%)
    pallas_call x1, Pallas kernels, shards(): pl.pallas_call(kernel, name='hyena', out_shape=pltpu.VMEM((rows, cols), B...  54.1 us

profile of v2, /device:TPU:9, one launch (start us, length us, event | category | flops | bytes accessed | tf_op | source)
XLA Modules:
  0.0 54.8 jit_solution(2381956086850663453)
XLA Ops:
  0.0 54.1 %hyena.1 = bf16[128,256]{1,0:T(8,128)(2,1)S(1)} custom-call(bf16[128,512]{1,0:T(8,128)(2,1)} %q_hbm.1, bf16[128,512]{1,0:T(8,128)(2,1)} %k_hbm.1, bf16[128,512]{1,0:T(8,128)(2,1)} %v_hbm.1, f32[3,3,512]{2,1,0:T(4,128)} %taps_hbm.1, f32[16,512]{1,0:T(8,128)} %bitcast.2, f32[16,512]{1,0:T(8,128)} %bitcast.3, bf16[512,4096]{1,0:T(8,128)(2,1)} %w_hbm.1), custom_call_target="tpu_custom_call" | custom-call | tf_op jit(solution)/shard_map/hyena/pallas_call | solution.py:358
  54.1 0.6 %copy.9 = bf16[128,256]{1,0:T(8,128)(2,1)} copy(bf16[128,256]{1,0:T(8,128)(2,1)S(1)} %hyena.1) | data formatting | bytes 131072

commit v3 on v2

--- a/solution.py
+++ b/solution.py
@@ -154,7 +154,7 @@
     for w_share in w_shares:
         w_share.start()
 
-    halo.wait()
+    halo.wait_recv()
     inside = jnp.where(ctx > 0, unpacked(halo_in[...]), 0.0)
     k_ext[6:8, :] = inside[2:4, :]
     v_ext[6:8, :] = inside[4:6, :]
@@ -208,7 +208,6 @@
     lax.fori_loop(0, channels // LANES, convolve, 0)
 
     for d in range(1, RUN):
-        z_copies[d - 1].wait_send()
         there = (z + d) % RUN
         put(z_out, z_in.at[there], z_send.at[d - 1], z_recv.at[there], along_z[d - 1]).wait_recv()
     before_me, total = jnp.zeros_like(step), jnp.zeros_like(step)
@@ -236,7 +235,6 @@
     for w_share in w_shares:
         w_share.wait()
     for d in range(1, rows_y):
-        pl.when(y + d < rows_y)(y_copies[d - 1].wait_send)
         there = (y + rows_y - d) % rows_y
         arrived = put(y_out, y_in.at[there], y_send.at[d - 1], y_recv.at[there], along_y[d - 1])
         pl.when(y >= d)(arrived.wait_recv)
@@ -287,55 +285,65 @@
         copy.start()
         g_copies.append(copy)
 
-    def share(c, b):
-        here = slice(c * chunk, (c + 1) * chunk)
-        value = jnp.dot(g_own[here, :], w_own[b], preferred_element_type=F32)
-        return value + jnp.dot(g_par[here, :], w_par[b], preferred_element_type=F32)
-
+    def share(b):
+        value = jnp.dot(g_own[...], w_own[b], preferred_element_type=F32)
+        return value + jnp.dot(g_par[...], w_par[b], preferred_element_type=F32)
+
+    for c in range(chunks):
+        g_copies[c].wait_recv()
     for part, h in enumerate((1 - half, half)):
-        for c in range(chunks):
-            if part == 0:
-                g_copies[c].wait()
-            for d in (2, 1, 3):
-                to = (x + d) % xs
-                x_out[part, c, d - 1] = share(c, to * 2 + h).astype(BF16)
+        copies = []
+        for d in (2, 1, 3):
+            to = (x + d) % xs
+            value = share(to * 2 + h).astype(BF16)
+            for c in range(chunks):
+                x_out[part, c, d - 1] = value[c * chunk : (c + 1) * chunk]
                 copy = put(
                     x_out.at[part, c, d - 1], x_in.at[part, c, d - 1],
                     x_send.at[part, c, d - 1], x_recv.at[part, c, d - 1], along_x[d - 1],
                 )
+                copies.append((c, copy))
+            copies[-chunks][1].start()
+        copies.sort(key=lambda item: item[0])
+        for c, copy in copies:
+            if c > 0:
                 copy.start()
-                x_copies.append(copy)
+            x_copies.append(copy)
     for part, h in enumerate((1 - half, half)):
-        for c in range(chunks):
-            x_keep[part, c] = share(c, x * 2 + h)
+        x_keep[part] = share(x * 2 + h)
 
     for part in range(2):
         for c in range(chunks):
-            for copy in x_copies[: xs - 1]:
-                copy.wait()
-            x_copies = x_copies[xs - 1 :]
+            at = (part * chunks + c) * (xs - 1)
+            for copy in x_copies[at : at + xs - 1]:
+                copy.wait_recv()
             for a in range(0, chunk, 16):
-                value = x_keep[part, c, a : a + 16, :]
+                here = slice(c * chunk + a, c * chunk + a + 16)
+                value = x_keep[part, here, :]
                 for d in range(1, xs):
                     value = value + x_in[part, c, d - 1, a : a + 16, :].astype(F32)
                 if part == 0:
                     h_out[c, a : a + 16, :] = value.astype(BF16)
                 else:
-                    x_keep[part, c, a : a + 16, :] = value
+                    x_keep[part, here, :] = value
             if part == 0:
                 copy = put(h_out.at[c], h_in.at[c], h_send.at[c], h_recv.at[c], other_half)
                 copy.start()
                 h_copies.append(copy)
 
     for c in range(chunks):
-        h_copies[c].wait()
+        h_copies[c].wait_recv()
         for a in range(0, chunk, 16):
-            value = x_keep[1, c, a : a + 16, :] + h_in[c, a : a + 16, :].astype(F32)
+            value = x_keep[1, c * chunk + a : c * chunk + a + 16, :] + h_in[c, a : a + 16, :].astype(F32)
             r = (c * chunk + a) // per
             for i in range(16 // per):
                 for g in range(cols // LANES):
                     part = value[i * per : (i + 1) * per, g * LANES : (g + 1) * LANES]
                     unperm[g, pl.ds(r + i, per, stride=BLOCK), :] = part
+    for copy in [halo] + z_copies + g_copies + x_copies + h_copies:
+        copy.wait_send()
+    for d in range(1, rows_y):
+        pl.when(y + d < rows_y)(y_copies[d - 1].wait_send)
     for g in range(cols // LANES):
         o_ref[:, g * LANES : (g + 1) * LANES] = unperm[g].astype(BF16)
 
@@ -394,7 +402,7 @@
                 stream, stream,
                 pltpu.VMEM((2, chunks, xs - 1, chunk, cols), BF16),
                 pltpu.VMEM((2, chunks, xs - 1, chunk, cols), BF16),
-                pltpu.VMEM((2, chunks, chunk, cols), F32),
+                pltpu.VMEM((2, rows, cols), F32),
                 pltpu.VMEM((chunks, chunk, cols), BF16),
                 pltpu.VMEM((chunks, chunk, cols), BF16),
                 pltpu.VMEM((cols // LANES, rows, LANES), F32),

time: 54.9 us -> 54.2 us (0.987)
  Pallas kernels: 54.1 us -> 53.4 us
    pallas_call x1, Pallas kernels: 54.1 us -> 53.4 us  [shards(): pl.pallas_call(kernel, name='hyena', out_shape=pltpu.VMEM((rows, cols), B...]
where the time goes in v3:
time: 54.2 us; the launch traced here: 54 us
  Pallas kernels  53.4 us (99%)
  local copies, waits for them, and re-layouts  0.63 us (1%)
    pallas_call x1, Pallas kernels, shards(): pl.pallas_call(kernel, name='hyena', out_shape=pltpu.VMEM((rows, cols), B...  53.4 us

profile of v3, /device:TPU:9, one launch (start us, length us, event | category | flops | bytes accessed | tf_op | source)
XLA Modules:
  0.0 54.0 jit_solution(7459828572179880932)
XLA Ops:
  0.0 53.4 %hyena.1 = bf16[128,256]{1,0:T(8,128)(2,1)S(1)} custom-call(bf16[128,512]{1,0:T(8,128)(2,1)} %q_hbm.1, bf16[128,512]{1,0:T(8,128)(2,1)} %k_hbm.1, bf16[128,512]{1,0:T(8,128)(2,1)} %v_hbm.1, f32[3,3,512]{2,1,0:T(4,128)} %taps_hbm.1, f32[16,512]{1,0:T(8,128)} %bitcast.2, f32[16,512]{1,0:T(8,128)} %bitcast.3, bf16[512,4096]{1,0:T(8,128)(2,1)} %w_hbm.1), custom_call_target="tpu_custom_call" | custom-call | tf_op jit(solution)/shard_map/hyena/pallas_call | solution.py:366
  53.4 0.6 %copy.9 = bf16[128,256]{1,0:T(8,128)(2,1)} copy(bf16[128,256]{1,0:T(8,128)(2,1)S(1)} %hyena.1) | data formatting | bytes 131072

commit v4 on v3

--- a/solution.py
+++ b/solution.py
@@ -64,22 +64,23 @@
     after, before = ((ctx + 1) % n_ctx, tp), ((ctx + n_ctx - 1) % n_ctx, tp)
 
     far_mate = (y * RUN + (z + RUN // 2) % RUN, other_half[1])
-    near_y = [d for d in range(1, rows_y) if min(d, rows_y - d) <= 2]
-    hop_y = [d for d in range(1, rows_y) if min(d, rows_y - d) == 2]
-    told = along_z + along_x + [other_core, before, far_mate] + [along_y[d - 1] for d in near_y]
-
-    barrier = pltpu.get_barrier_semaphore()
-    for peer in told:
-        pl.semaphore_signal(barrier, inc=1, device_id=peer, device_id_type=MESH)
+    near_y, hop_y = ([d for d in range(1, rows_y) if min(d, rows_y - d) == reach] for reach in (1, 2))
+    near_x = [d for d in range(1, xs) if min(d, xs - d) == 1]
+    told = along_z + [other_core, before, far_mate] + [along_y[d - 1] for d in near_y] + [along_x[d - 1] for d in near_x]
 
     loads = [
         pltpu.make_async_copy(src, dst, in_sem.at[i])
         for i, (src, dst) in enumerate(
-            [(q_hbm, q_in), (k_hbm, k_in), (v_hbm, v_in), (taps_hbm, taps), (rate_hbm, rate_in), (resid_hbm, resid_in)]
+            [(k_hbm, k_in), (v_hbm, v_in), (taps_hbm, taps), (rate_hbm, rate_in), (q_hbm, q_in), (resid_hbm, resid_in)]
         )
     ]
     for load in loads:
         load.start()
+
+    barrier = pltpu.get_barrier_semaphore()
+    for peer in told:
+        pl.semaphore_signal(barrier, inc=1, device_id=peer, device_id_type=MESH)
+
     blocks = 2 * xs
     w_loads = [
         pltpu.make_async_copy(
@@ -147,8 +148,10 @@
     z_copies = [put(z_out, z_in.at[z], z_send.at[d - 1], z_recv.at[z], along_z[d - 1]) for d in range(1, RUN)]
     for copy in z_copies:
         copy.start()
-    for d in hop_y:
-        pl.semaphore_signal(ring_sem, inc=1, device_id=along_y[d - 1], device_id_type=MESH)
+    for d in near_y:
+        pl.semaphore_signal(ring_sem.at[0], inc=1, device_id=along_y[d - 1], device_id_type=MESH)
+    for d in near_x:
+        pl.semaphore_signal(ring_sem.at[1], inc=1, device_id=along_x[d - 1], device_id_type=MESH)
     halo = put(halo_out, halo_in, halo_sem.at[0], halo_sem.at[1], after)
     halo.start()
     for w_share in w_shares:
@@ -207,6 +210,10 @@
 
     lax.fori_loop(0, channels // LANES, convolve, 0)
 
+    pl.semaphore_wait(ring_sem.at[0], len(near_y))
+    for d in hop_y:
+        pl.semaphore_signal(ring_sem.at[2], inc=1, device_id=along_y[d - 1], device_id_type=MESH)
+    pl.semaphore_wait(ring_sem.at[1], len(near_x))
     for d in range(1, RUN):
         there = (z + d) % RUN
         put(z_out, z_in.at[there], z_send.at[d - 1], z_recv.at[there], along_z[d - 1]).wait_recv()
@@ -223,9 +230,9 @@
     row_edges = [edges[0][0:2], edges[0][2:4], edges[RUN - 1][4:6], edges[RUN - 1][6:8]]
     y_out[:, channels:] = packed(row_edges)
     y_in[y] = y_out[...]
-    pl.semaphore_wait(ring_sem, len(hop_y))
+    pl.semaphore_wait(ring_sem.at[2], len(hop_y))
     y_copies = [put(y_out, y_in.at[y], y_send.at[d - 1], y_recv.at[y], along_y[d - 1]) for d in range(1, rows_y)]
-    for d in sorted(range(1, rows_y), key=lambda d: -min(d, rows_y - d)):
+    for d in range(1, rows_y):
         pl.when(y + d < rows_y)(y_copies[d - 1].start)
     row_decay = jnp.exp(rate[...] * (-1.0 * rows * RUN))
     row_gain = jnp.exp(rate[...] * (2.0 - rows * RUN))
@@ -291,6 +298,7 @@
 
     for c in range(chunks):
         g_copies[c].wait_recv()
+    waiting = []
     for part, h in enumerate((1 - half, half)):
         copies = []
         for d in (2, 1, 3):
@@ -303,14 +311,18 @@
                     x_send.at[part, c, d - 1], x_recv.at[part, c, d - 1], along_x[d - 1],
                 )
                 copies.append((c, copy))
-            copies[-chunks][1].start()
+            if part == 0:
+                copies[-chunks][1].start()
         copies.sort(key=lambda item: item[0])
         for c, copy in copies:
-            if c > 0:
+            if part == 0 and c > 0:
                 copy.start()
+            if part == 1:
+                waiting.append(copy)
             x_copies.append(copy)
-    for part, h in enumerate((1 - half, half)):
-        x_keep[part] = share(x * 2 + h)
+        if part == 0:
+            x_keep[0] = share(x * 2 + h)
+    x_keep[1] = share(x * 2 + half)
 
     for part in range(2):
         for c in range(chunks):
@@ -330,6 +342,9 @@
                 copy = put(h_out.at[c], h_in.at[c], h_send.at[c], h_recv.at[c], other_half)
                 copy.start()
                 h_copies.append(copy)
+                if c == chunks - 1:
+                    for copy in waiting:
+                        copy.start()
 
     for c in range(chunks):
         h_copies[c].wait_recv()
@@ -414,7 +429,7 @@
                 sem((chunks,)), sem((chunks,)),
                 sem((2, chunks, xs - 1)), sem((2, chunks, xs - 1)),
                 sem((chunks,)), sem((chunks,)),
-                pltpu.SemaphoreType.REGULAR,
+                pltpu.SemaphoreType.REGULAR((3,)),
             ],
             compiler_params=pltpu.CompilerParams(
                 collective_id=0, has_side_effects=True, vmem_limit_bytes=62 * 1024 * 1024

time: 54.2 us -> 55.8 us (1.030)
  the two profiles are of different devices: /device:TPU:9 before, /device:TPU:49 now
where the time goes in v4:
time: 55.8 us; the launch traced here: 55.6 us
  Pallas kernels  55 us (99%)
  local copies, waits for them, and re-layouts  0.63 us (1%)
    pallas_call x1, Pallas kernels, shards(): pl.pallas_call(kernel, name='hyena', out_shape=pltpu.VMEM((rows, cols), B...  55 us

profile of v4, /device:TPU:49, one launch (start us, length us, event | category | flops | bytes accessed | tf_op | source)
XLA Modules:
  0.0 55.6 jit_solution(6216516803873684263)
XLA Ops:
  0.0 55.0 %hyena.1 = bf16[128,256]{1,0:T(8,128)(2,1)S(1)} custom-call(bf16[128,512]{1,0:T(8,128)(2,1)} %q_hbm.1, bf16[128,512]{1,0:T(8,128)(2,1)} %k_hbm.1, bf16[128,512]{1,0:T(8,128)(2,1)} %v_hbm.1, f32[3,3,512]{2,1,0:T(4,128)} %taps_hbm.1, f32[16,512]{1,0:T(8,128)} %bitcast.2, f32[16,512]{1,0:T(8,128)} %bitcast.3, bf16[512,4096]{1,0:T(8,128)(2,1)} %w_hbm.1), custom_call_target="tpu_custom_call" | custom-call | tf_op jit(solution)/shard_map/hyena/pallas_call | solution.py:381
  55.0 0.6 %copy.9 = bf16[128,256]{1,0:T(8,128)(2,1)} copy(bf16[128,256]{1,0:T(8,128)(2,1)S(1)} %hyena.1) | data formatting | bytes 131072

commit v5 on v4

--- a/solution.py
+++ b/solution.py
@@ -64,9 +64,9 @@
     after, before = ((ctx + 1) % n_ctx, tp), ((ctx + n_ctx - 1) % n_ctx, tp)
 
     far_mate = (y * RUN + (z + RUN // 2) % RUN, other_half[1])
-    near_y, hop_y = ([d for d in range(1, rows_y) if min(d, rows_y - d) == reach] for reach in (1, 2))
-    near_x = [d for d in range(1, xs) if min(d, xs - d) == 1]
-    told = along_z + [other_core, before, far_mate] + [along_y[d - 1] for d in near_y] + [along_x[d - 1] for d in near_x]
+    near_y = [d for d in range(1, rows_y) if min(d, rows_y - d) <= 2]
+    hop_y = [d for d in range(1, rows_y) if min(d, rows_y - d) == 2]
+    told = along_z + along_x + [other_core, before, far_mate] + [along_y[d - 1] for d in near_y]
 
     loads = [
         pltpu.make_async_copy(src, dst, in_sem.at[i])
@@ -148,21 +148,12 @@
     z_copies = [put(z_out, z_in.at[z], z_send.at[d - 1], z_recv.at[z], along_z[d - 1]) for d in range(1, RUN)]
     for copy in z_copies:
         copy.start()
-    for d in near_y:
-        pl.semaphore_signal(ring_sem.at[0], inc=1, device_id=along_y[d - 1], device_id_type=MESH)
-    for d in near_x:
-        pl.semaphore_signal(ring_sem.at[1], inc=1, device_id=along_x[d - 1], device_id_type=MESH)
+    for d in hop_y:
+        pl.semaphore_signal(ring_sem, inc=1, device_id=along_y[d - 1], device_id_type=MESH)
     halo = put(halo_out, halo_in, halo_sem.at[0], halo_sem.at[1], after)
     halo.start()
     for w_share in w_shares:
         w_share.start()
-
-    halo.wait_recv()
-    inside = jnp.where(ctx > 0, unpacked(halo_in[...]), 0.0)
-    k_ext[6:8, :] = inside[2:4, :]
-    v_ext[6:8, :] = inside[4:6, :]
-    p_ext[0:8, :] = product(0, 8)
-    heads[...] = step * p_ext[0:1, :] + p_ext[1:2, :]
 
     def boundary(last, first):
         value = [1.0, 1.0]
@@ -188,32 +179,7 @@
         for b in range(per):
             decay_b[g, pl.ds(b, modes, stride=per), :] = step[:, lanes]
             gain_b[g, pl.ds(b, modes, stride=per), :] = first_gain[:, lanes]
-        q_ext[g, 6:8, :] = inside[0:2, lanes]
-        for a in range(0, rows, 16):
-            q_ext[g, 8 + a : 24 + a, :] = q_in[a : a + 16, lanes].astype(F32)
-            p_group[g, a : a + 16, :] = p_ext[a : a + 16, lanes]
-        for r in range(BLOCK):
-            total = taps[0, 0:1, lanes] * q_ext[g, pl.ds(8 + r, per, stride=BLOCK), :]
-            total = total + taps[0, 1:2, lanes] * q_ext[g, pl.ds(7 + r, per, stride=BLOCK), :]
-            total = total + taps[0, 2:3, lanes] * q_ext[g, pl.ds(6 + r, per, stride=BLOCK), :]
-            q_feat[r * per : (r + 1) * per, lanes] = total
-
-    def convolve(group, carry):
-        lanes = pl.ds(pl.multiple_of(group * LANES, LANES), LANES)
-        inputs = [p_group[group, pl.ds(r, per, stride=BLOCK), :] for r in range(BLOCK)]
-        for r in range(BLOCK):
-            total = response[0:1, lanes] * inputs[r]
-            for k in range(1, r + 1):
-                total = total + response[k : k + 1, lanes] * inputs[r - k]
-            local[r * per : (r + 1) * per, lanes] = total
-        return carry
-
-    lax.fori_loop(0, channels // LANES, convolve, 0)
-
-    pl.semaphore_wait(ring_sem.at[0], len(near_y))
-    for d in hop_y:
-        pl.semaphore_signal(ring_sem.at[2], inc=1, device_id=along_y[d - 1], device_id_type=MESH)
-    pl.semaphore_wait(ring_sem.at[1], len(near_x))
+
     for d in range(1, RUN):
         there = (z + d) % RUN
         put(z_out, z_in.at[there], z_send.at[d - 1], z_recv.at[there], along_z[d - 1]).wait_recv()
@@ -230,17 +196,42 @@
     row_edges = [edges[0][0:2], edges[0][2:4], edges[RUN - 1][4:6], edges[RUN - 1][6:8]]
     y_out[:, channels:] = packed(row_edges)
     y_in[y] = y_out[...]
-    pl.semaphore_wait(ring_sem.at[2], len(hop_y))
+    pl.semaphore_wait(ring_sem, len(hop_y))
     y_copies = [put(y_out, y_in.at[y], y_send.at[d - 1], y_recv.at[y], along_y[d - 1]) for d in range(1, rows_y)]
-    for d in range(1, rows_y):
+    for d in sorted(range(1, rows_y), key=lambda d: (d != 1, -min(d, rows_y - d))):
         pl.when(y + d < rows_y)(y_copies[d - 1].start)
+    halo.wait_recv()
+    inside = jnp.where(ctx > 0, unpacked(halo_in[...]), 0.0)
+    k_ext[6:8, :] = inside[2:4, :]
+    v_ext[6:8, :] = inside[4:6, :]
+    p_ext[0:8, :] = product(0, 8)
+    heads[...] = step * p_ext[0:1, :] + p_ext[1:2, :]
+    for g, lanes in enumerate(groups):
+        q_ext[g, 6:8, :] = inside[0:2, lanes]
+        for a in range(0, rows, 16):
+            q_ext[g, 8 + a : 24 + a, :] = q_in[a : a + 16, lanes].astype(F32)
+            p_group[g, a : a + 16, :] = p_ext[a : a + 16, lanes]
+        for r in range(BLOCK):
+            total = taps[0, 0:1, lanes] * q_ext[g, pl.ds(8 + r, per, stride=BLOCK), :]
+            total = total + taps[0, 1:2, lanes] * q_ext[g, pl.ds(7 + r, per, stride=BLOCK), :]
+            total = total + taps[0, 2:3, lanes] * q_ext[g, pl.ds(6 + r, per, stride=BLOCK), :]
+            q_feat[r * per : (r + 1) * per, lanes] = total
+
+    def convolve(group, carry):
+        lanes = pl.ds(pl.multiple_of(group * LANES, LANES), LANES)
+        inputs = [p_group[group, pl.ds(r, per, stride=BLOCK), :] for r in range(BLOCK)]
+        for r in range(BLOCK):
+            total = response[0:1, lanes] * inputs[r]
+            for k in range(1, r + 1):
+                total = total + response[k : k + 1, lanes] * inputs[r - k]
+            local[r * per : (r + 1) * per, lanes] = total
+        return carry
+
+    lax.fori_loop(0, channels // LANES, convolve, 0)
+
     row_decay = jnp.exp(rate[...] * (-1.0 * rows * RUN))
     row_gain = jnp.exp(rate[...] * (2.0 - rows * RUN))
     my_gain = jnp.exp(rate[...] * (2.0 - rows * z.astype(F32)))
-    for w_load in w_loads:
-        w_load.wait()
-    for w_share in w_shares:
-        w_share.wait()
     for d in range(1, rows_y):
         there = (y + rows_y - d) % rows_y
         arrived = put(y_out, y_in.at[there], y_send.at[d - 1], y_recv.at[there], along_y[d - 1])
@@ -296,6 +287,10 @@
         value = jnp.dot(g_own[...], w_own[b], preferred_element_type=F32)
         return value + jnp.dot(g_par[...], w_par[b], preferred_element_type=F32)
 
+    for w_load in w_loads:
+        w_load.wait()
+    for w_share in w_shares:
+        w_share.wait()
     for c in range(chunks):
         g_copies[c].wait_recv()
     waiting = []
@@ -429,7 +424,7 @@
                 sem((chunks,)), sem((chunks,)),
                 sem((2, chunks, xs - 1)), sem((2, chunks, xs - 1)),
                 sem((chunks,)), sem((chunks,)),
-                pltpu.SemaphoreType.REGULAR((3,)),
+                pltpu.SemaphoreType.REGULAR,
             ],
             compiler_params=pltpu.CompilerParams(
                 collective_id=0, has_side_effects=True, vmem_limit_bytes=62 * 1024 * 1024

time: 55.8 us -> 51.4 us (0.921)
  the two profiles are of different devices: /device:TPU:49 before, /device:TPU:113 now
where the time goes in v5:
time: 51.4 us; the launch traced here: 51.2 us
  Pallas kernels  50.6 us (98%)
  local copies, waits for them, and re-layouts  0.63 us (1%)
    pallas_call x1, Pallas kernels, shards(): pl.pallas_call(kernel, name='hyena', out_shape=pltpu.VMEM((rows, cols), B...  50.6 us

profile of v5, /device:TPU:113, one launch (start us, length us, event | category | flops | bytes accessed | tf_op | source)
XLA Modules:
  0.0 51.2 jit_solution(12387360453867254785)
XLA Ops:
  0.0 50.6 %hyena.1 = bf16[128,256]{1,0:T(8,128)(2,1)S(1)} custom-call(bf16[128,512]{1,0:T(8,128)(2,1)} %q_hbm.1, bf16[128,512]{1,0:T(8,128)(2,1)} %k_hbm.1, bf16[128,512]{1,0:T(8,128)(2,1)} %v_hbm.1, f32[3,3,512]{2,1,0:T(4,128)} %taps_hbm.1, f32[16,512]{1,0:T(8,128)} %bitcast.2, f32[16,512]{1,0:T(8,128)} %bitcast.3, bf16[512,4096]{1,0:T(8,128)(2,1)} %w_hbm.1), custom_call_target="tpu_custom_call" | custom-call | tf_op jit(solution)/shard_map/hyena/pallas_call | solution.py:376
  50.6 0.6 %copy.9 = bf16[128,256]{1,0:T(8,128)(2,1)} copy(bf16[128,256]{1,0:T(8,128)(2,1)S(1)} %hyena.1) | data formatting | bytes 131072

commit v6 on v5

--- a/solution.py
+++ b/solution.py
@@ -180,12 +180,11 @@
             decay_b[g, pl.ds(b, modes, stride=per), :] = step[:, lanes]
             gain_b[g, pl.ds(b, modes, stride=per), :] = first_gain[:, lanes]
 
-    for d in range(1, RUN):
-        there = (z + d) % RUN
-        put(z_out, z_in.at[there], z_send.at[d - 1], z_recv.at[there], along_z[d - 1]).wait_recv()
     before_me, total = jnp.zeros_like(step), jnp.zeros_like(step)
-    edges = [unpacked(z_in[i, :, channels:]) for i in range(RUN)]
+    edges = []
     for i in range(RUN):
+        pl.when(z != i)(put(z_out, z_in.at[i], z_send.at[0], z_recv.at[i], along_z[0]).wait_recv)
+        edges.append(unpacked(z_in[i, :, channels:]))
         value = z_in[i, :, :channels].astype(F32)
         if i > 0:
             value = value + head_gain * boundary(edges[i - 1], edges[i])
@@ -232,14 +231,11 @@
     row_decay = jnp.exp(rate[...] * (-1.0 * rows * RUN))
     row_gain = jnp.exp(rate[...] * (2.0 - rows * RUN))
     my_gain = jnp.exp(rate[...] * (2.0 - rows * z.astype(F32)))
-    for d in range(1, rows_y):
-        there = (y + rows_y - d) % rows_y
-        arrived = put(y_out, y_in.at[there], y_send.at[d - 1], y_recv.at[there], along_y[d - 1])
-        pl.when(y >= d)(arrived.wait_recv)
     state = jnp.zeros_like(step)
     last = jnp.zeros((8, channels), F32)
     row_heads = jnp.zeros_like(step)
     for i in range(rows_y):
+        pl.when(i < y)(put(y_out, y_in.at[i], y_send.at[0], y_recv.at[i], along_y[0]).wait_recv)
         edge = unpacked(y_in[i, :, channels:])
         head = boundary(last, edge)
         row_heads = jnp.where(i == y, head, row_heads)

time: 51.4 us -> 51.3 us (level)
  no operation moved by 1% of the time
where the time goes in v6:
time: 51.3 us; the launch traced here: 51.1 us
  Pallas kernels  50.5 us (98%)
  local copies, waits for them, and re-layouts  0.63 us (1%)
    pallas_call x1, Pallas kernels, shards(): pl.pallas_call(kernel, name='hyena', out_shape=pltpu.VMEM((rows, cols), B...  50.5 us

profile of v6, /device:TPU:113, one launch (start us, length us, event | category | flops | bytes accessed | tf_op | source)
XLA Modules:
  0.0 51.1 jit_solution(7620794806694564610)
XLA Ops:
  0.0 50.5 %hyena.1 = bf16[128,256]{1,0:T(8,128)(2,1)S(1)} custom-call(bf16[128,512]{1,0:T(8,128)(2,1)} %q_hbm.1, bf16[128,512]{1,0:T(8,128)(2,1)} %k_hbm.1, bf16[128,512]{1,0:T(8,128)(2,1)} %v_hbm.1, f32[3,3,512]{2,1,0:T(4,128)} %taps_hbm.1, f32[16,512]{1,0:T(8,128)} %bitcast.2, f32[16,512]{1,0:T(8,128)} %bitcast.3, bf16[512,4096]{1,0:T(8,128)(2,1)} %w_hbm.1), custom_call_target="tpu_custom_call" | custom-call | tf_op jit(solution)/shard_map/hyena/pallas_call | solution.py:372
  50.5 0.6 %copy.9 = bf16[128,256]{1,0:T(8,128)(2,1)} copy(bf16[128,256]{1,0:T(8,128)(2,1)S(1)} %hyena.1) | data formatting | bytes 131072

commit v7 on v6

--- a/solution.py
+++ b/solution.py
@@ -65,6 +65,7 @@
 
     far_mate = (y * RUN + (z + RUN // 2) % RUN, other_half[1])
     near_y = [d for d in range(1, rows_y) if min(d, rows_y - d) <= 2]
+    far_y = [d for d in range(1, rows_y) if d not in near_y]
     hop_y = [d for d in range(1, rows_y) if min(d, rows_y - d) == 2]
     told = along_z + along_x + [other_core, before, far_mate] + [along_y[d - 1] for d in near_y]
 
@@ -80,6 +81,12 @@
     barrier = pltpu.get_barrier_semaphore()
     for peer in told:
         pl.semaphore_signal(barrier, inc=1, device_id=peer, device_id_type=MESH)
+
+    @pl.when(z < RUN // 2)
+    def _():
+        for d in far_y:
+            pl.semaphore_signal(barrier, inc=1, device_id=along_y[d - 1], device_id_type=MESH)
+
 
     blocks = 2 * xs
     w_loads = [
@@ -144,12 +151,16 @@
     z_out[:, channels:] = packed([k_first[0:2], v_first[0:2], k_last, v_last])
     z_in[z] = z_out[...]
     halo_out[...] = packed([q_last, k_last, v_last, jnp.zeros_like(v_last)])
-    pl.semaphore_wait(barrier, len(told))
+    pl.semaphore_wait(barrier, len(told) + jnp.where(z < RUN // 2, len(far_y), 0))
     z_copies = [put(z_out, z_in.at[z], z_send.at[d - 1], z_recv.at[z], along_z[d - 1]) for d in range(1, RUN)]
     for copy in z_copies:
         copy.start()
-    for d in hop_y:
-        pl.semaphore_signal(ring_sem, inc=1, device_id=along_y[d - 1], device_id_type=MESH)
+
+    @pl.when(z >= RUN // 2)
+    def _():
+        for d in hop_y:
+            pl.semaphore_signal(ring_sem, inc=1, device_id=along_y[d - 1], device_id_type=MESH)
+
     halo = put(halo_out, halo_in, halo_sem.at[0], halo_sem.at[1], after)
     halo.start()
     for w_share in w_shares:
@@ -195,7 +206,10 @@
     row_edges = [edges[0][0:2], edges[0][2:4], edges[RUN - 1][4:6], edges[RUN - 1][6:8]]
     y_out[:, channels:] = packed(row_edges)
     y_in[y] = y_out[...]
-    pl.semaphore_wait(ring_sem, len(hop_y))
+    @pl.when(z >= RUN // 2)
+    def _():
+        pl.semaphore_wait(ring_sem, len(hop_y))
+
     y_copies = [put(y_out, y_in.at[y], y_send.at[d - 1], y_recv.at[y], along_y[d - 1]) for d in range(1, rows_y)]
     for d in sorted(range(1, rows_y), key=lambda d: (d != 1, -min(d, rows_y - d))):
         pl.when(y + d < rows_y)(y_copies[d - 1].start)

time: 51.3 us -> 51.3 us (level)
  no operation moved by 1% of the time
where the time goes in v7:
time: 51.3 us; the launch traced here: 51.1 us
  Pallas kernels  50.5 us (98%)
  local copies, waits for them, and re-layouts  0.63 us (1%)
    pallas_call x1, Pallas kernels, shards(): pl.pallas_call(kernel, name='hyena', out_shape=pltpu.VMEM((rows, cols), B...  50.5 us

profile of v7, /device:TPU:113, one launch (start us, length us, event | category | flops | bytes accessed | tf_op | source)
XLA Modules:
  0.0 51.1 jit_solution(4778884910150900816)
XLA Ops:
  0.0 50.5 %hyena.1 = bf16[128,256]{1,0:T(8,128)(2,1)S(1)} custom-call(bf16[128,512]{1,0:T(8,128)(2,1)} %q_hbm.1, bf16[128,512]{1,0:T(8,128)(2,1)} %k_hbm.1, bf16[128,512]{1,0:T(8,128)(2,1)} %v_hbm.1, f32[3,3,512]{2,1,0:T(4,128)} %taps_hbm.1, f32[16,512]{1,0:T(8,128)} %bitcast.2, f32[16,512]{1,0:T(8,128)} %bitcast.3, bf16[512,4096]{1,0:T(8,128)(2,1)} %w_hbm.1), custom_call_target="tpu_custom_call" | custom-call | tf_op jit(solution)/shard_map/hyena/pallas_call | solution.py:386
  50.5 0.6 %copy.9 = bf16[128,256]{1,0:T(8,128)(2,1)} copy(bf16[128,256]{1,0:T(8,128)(2,1)S(1)} %hyena.1) | data formatting | bytes 131072
